TPU v7x, 32 devices: a whole 2x2x4 slice. The times are simulated.
32 devices in a mesh: dp: 2 (over x), seq: 8 (over z, y), mp: 2 (over core).
Axes of the slice: x: 2, y: 2, z: 4, core: 2. Of those that a mesh axis runs over, the one named last changes fastest.
Arguments:
- tokens: bfloat16 [4, 2048, 512], P('dp', ('seq', 'mp')), may hold values from -6 to 6
- segments: int32 [4, 2048], P('dp', ('seq', 'mp')), may hold values from 0 to 16, as said below
- timesteps: int32 [4], P('dp'), may hold values from 0 to 999
- step_table: bfloat16 [1000, 512], replicated, may hold values from -3 to 3
- first_gain: float32 [512], replicated, may hold values from 0.5 to 1.5
- first_shift: float32 [512], replicated, may hold values from -3 to 3
- query_weight: bfloat16 [512, 512], P(None, 'mp'), may hold values from -0.25 to 0.25
- query_bias: bfloat16 [512], P('mp'), may hold values from -3 to 3
- key_weight: bfloat16 [512, 512], P(None, 'mp'), may hold values from -0.25 to 0.25
- value_weight: bfloat16 [512, 512], P(None, 'mp'), may hold values from -0.25 to 0.25
- value_bias: bfloat16 [512], P('mp'), may hold values from -3 to 3
- out_weight: bfloat16 [512, 512], P('mp'), may hold values from -2 to 2
- out_bias: bfloat16 [512], replicated, may hold values from -3 to 3
- second_gain: float32 [512], replicated, may hold values from 0.5 to 1.5
- second_shift: float32 [512], replicated, may hold values from -3 to 3
- up_weight: bfloat16 [512, 2048], P(None, 'mp'), may hold values from -0.25 to 0.25
- up_bias: bfloat16 [2048], P('mp'), may hold values from -3 to 3
- down_weight: bfloat16 [2048, 512], P('mp'), may hold values from -0.25 to 0.25
- down_bias: bfloat16 [512], replicated, may hold values from -3 to 3
- cotangent: bfloat16 [4, 2048, 512], P('dp', ('seq', 'mp')), may hold values from -6 to 6
Outputs:
- result: bfloat16 [4, 2048, 512], P('dp', ('seq', 'mp'))
- token_grad: float32 [4, 2048, 512], P('dp', ('seq', 'mp'))
- table_grad: float32 [1000, 512], replicated
- first_gain_grad: float32 [512], replicated
- first_shift_grad: float32 [512], replicated
- query_weight_grad: float32 [512, 512], P(None, 'mp')
- query_bias_grad: float32 [512], P('mp')
- key_weight_grad: float32 [512, 512], P(None, 'mp')
- value_weight_grad: float32 [512, 512], P(None, 'mp')
- value_bias_grad: float32 [512], P('mp')
- out_weight_grad: float32 [512, 512], P('mp')
- out_bias_grad: float32 [512], replicated
- second_gain_grad: float32 [512], replicated
- second_shift_grad: float32 [512], replicated
- up_weight_grad: float32 [512, 2048], P(None, 'mp')
- up_bias_grad: float32 [2048], P('mp')
- down_weight_grad: float32 [2048, 512], P('mp')
- down_bias_grad: float32 [512], replicated
Inputs may be any that keep to these rules, and one draw needn't show every extreme that they name: `segments`: along each row the ids never fall before the padding; 0 marks padding, which fills the last 32 to 128 characters of every row and nothing else.
All inputs are finite; a program needn't handle non-finite values.
Results may differ from a plain program's by a relative error of at most 0.03.
Values may be sent and summed in bfloat16 or wider, within the bound.
A program may use at most 128 MiB of HBM per device.

v0:
```python
import math

import jax
import jax.numpy as jnp
from jax import lax
from jax.sharding import PartitionSpec as P

HEAD_DIM = 64


masked = -1e30
highest = lax.Precision.HIGHEST


def layer_norm(value, gain, shift):
    average = jnp.mean(value, axis=-1, keepdims=True)
    centred = value - average
    spread = jnp.mean(centred * centred, axis=-1, keepdims=True)
    return centred * lax.rsqrt(spread + 1e-05) * gain + shift


def gelu_curve(value):
    return jax.nn.gelu(value, approximate=True)


def tokens_dot(left, right):
    return jnp.einsum("rla,rlb->ab", left, right, preferred_element_type=jnp.float32)


def local(
    tokens,
    segments,
    timesteps,
    step_table,
    first_gain,
    first_shift,
    query_weight,
    query_bias,
    key_weight,
    value_weight,
    value_bias,
    out_weight,
    out_bias,
    second_gain,
    second_shift,
    up_weight,
    up_bias,
    down_weight,
    down_bias,
    cotangent,
):
    bfloat = jnp.bfloat16
    rows_here = tokens.shape[0]
    local_width = query_weight.shape[1]
    heads_here = local_width // HEAD_DIM
    scale = 1.0 / math.sqrt(HEAD_DIM)
    table_ids = jnp.arange(step_table.shape[0], dtype=jnp.int32)
    picks = (timesteps[:, None] == table_ids[None, :]).astype(jnp.float32)
    row_embed = jnp.dot(picks.astype(bfloat), step_table, preferred_element_type=jnp.float32)
    hidden = tokens.astype(jnp.float32) + row_embed[:, None, :]
    normed = layer_norm(hidden, first_gain, first_shift).astype(bfloat)
    normed_all, seg_all = (
        lax.all_gather(normed, "mp", axis=1, tiled=True),
        lax.all_gather(segments.astype(bfloat), "mp", axis=1, tiled=True),
    )
    section = normed_all.shape[1]
    live = (seg_all > 0).astype(bfloat)
    proj_weight = jnp.concatenate([query_weight, key_weight, value_weight], axis=1)
    proj_bias = jnp.concatenate([query_bias, jnp.zeros_like(query_bias), value_bias])
    projected = (
        jnp.dot(normed_all, proj_weight, preferred_element_type=jnp.float32) + proj_bias
    ).astype(bfloat)
    query = projected[:, :, :local_width].reshape(rows_here, section, heads_here, HEAD_DIM)
    keys = projected[:, :, local_width : 2 * local_width]
    values = projected[:, :, 2 * local_width :]

    def piece_rows(piece):
        key_piece, value_piece, seg_piece = piece
        count = key_piece.shape[1]
        return (
            count,
            key_piece.reshape(rows_here, count, heads_here, HEAD_DIM),
            value_piece.reshape(rows_here, count, heads_here, HEAD_DIM),
            seg_piece,
        )

    def row_scores(query_row, seg_query, key_row, seg_key):
        scores = (
            jnp.einsum("qhe,khe->hqk", query_row, key_row, preferred_element_type=jnp.float32)
            * scale
        )
        allowed = (seg_query[:, None] == seg_key[None, :])[None]
        return (jnp.where(allowed, scores, masked), allowed)

    start_state = (
        jnp.full((rows_here, heads_here, section), masked, jnp.float32),
        jnp.zeros((rows_here, heads_here, section), jnp.float32),
        jnp.zeros((rows_here, section, heads_here, HEAD_DIM), jnp.float32),
    )
    count, key_piece, value_piece, seg_piece = piece_rows(
        (
            lax.all_gather(keys, "seq", axis=1, tiled=True),
            lax.all_gather(values, "seq", axis=1, tiled=True),
            lax.all_gather(seg_all, "seq", axis=1, tiled=True),
        )
    )

    def attend_one_row(inputs):
        top_row, total_row, summed_row, query_row, seg_query, key_row, value_row, seg_key = inputs
        scores, allowed = row_scores(query_row, seg_query, key_row, seg_key)
        new_top = jnp.maximum(top_row, jnp.max(scores, axis=-1))
        weights = jnp.where(allowed, jnp.exp(scores - new_top[:, :, None]), 0.0)
        factor = jnp.exp(top_row - new_top)
        total_row = total_row * factor + jnp.sum(weights, axis=-1)
        summed_row = summed_row * jnp.transpose(factor)[:, :, None] + jnp.einsum(
            "hqk,khe->qhe", weights.astype(bfloat), value_row, preferred_element_type=jnp.float32
        )
        return (new_top, total_row, summed_row)

    top, total, summed = lax.map(
        attend_one_row,
        (
            start_state[0],
            start_state[1],
            start_state[2],
            query,
            seg_all,
            key_piece,
            value_piece,
            seg_piece,
        ),
    )
    attended = summed / jnp.transpose(total, (0, 2, 1))[:, :, :, None]
    log_total = top + jnp.log(total)
    mixed = (attended.reshape(rows_here, section, local_width) * live[:, :, None]).astype(bfloat)
    branch = jnp.dot(mixed, out_weight, preferred_element_type=jnp.float32)
    residual = (
        hidden
        + lax.psum_scatter(
            branch.astype(jnp.bfloat16), "mp", scatter_dimension=1, tiled=True
        ).astype(jnp.float32)
        + out_bias
    )
    normed_second = layer_norm(residual, second_gain, second_shift).astype(bfloat)
    normed_second_all = lax.all_gather(normed_second, "mp", axis=1, tiled=True)
    inner = jnp.dot(normed_second_all, up_weight, preferred_element_type=jnp.float32) + up_bias
    activated = gelu_curve(inner).astype(bfloat)
    unit_part = jnp.dot(activated, down_weight, preferred_element_type=jnp.float32)
    result = (
        residual
        + lax.psum_scatter(
            unit_part.astype(jnp.bfloat16), "mp", scatter_dimension=1, tiled=True
        ).astype(jnp.float32)
        + down_bias
    ).astype(bfloat)
    cotangent_all = lax.all_gather(cotangent, "mp", axis=1, tiled=True)
    grad_activated = jnp.einsum(
        "rld,fd->rlf", cotangent_all, down_weight, preferred_element_type=jnp.float32
    )
    unused, gelu_back = jax.vjp(gelu_curve, inner)
    grad_inner = gelu_back(grad_activated)[0].astype(bfloat)
    grad_normed_second = lax.psum_scatter(
        jnp.einsum("rlf,df->rld", grad_inner, up_weight, preferred_element_type=jnp.float32).astype(
            jnp.bfloat16
        ),
        "mp",
        scatter_dimension=1,
        tiled=True,
    ).astype(jnp.float32)
    unit_grads = (
        tokens_dot(normed_second_all, grad_inner),
        jnp.sum(grad_inner, axis=(0, 1), dtype=jnp.float32),
        tokens_dot(activated, cotangent_all),
    )
    unused, second_back = jax.vjp(layer_norm, residual, second_gain, second_shift)
    grad_from_norm, grad_gain_second, grad_shift_second = second_back(grad_normed_second)
    grad_residual = cotangent.astype(jnp.float32) + grad_from_norm
    branch_grad = lax.all_gather(grad_residual.astype(bfloat), "mp", axis=1, tiled=True)
    grad_out = tokens_dot(mixed, branch_grad)
    grad_mixed = (
        jnp.einsum(
            "rld,wd->rlw", branch_grad, out_weight, preferred_element_type=jnp.float32
        ).astype(bfloat)
        * live[:, :, None]
    )
    grad_heads = grad_mixed.reshape(rows_here, section, heads_here, HEAD_DIM)
    delta = jnp.transpose(jnp.sum(grad_heads * attended, axis=-1), (0, 2, 1))
    count, key_piece, value_piece, seg_piece = piece_rows(
        (
            lax.all_gather(keys, "seq", axis=1, tiled=True),
            lax.all_gather(values, "seq", axis=1, tiled=True),
            lax.all_gather(seg_all, "seq", axis=1, tiled=True),
        )
    )

    def back_one_row(inputs):
        query_row, seg_query, lse_row, delta_row, heads_row, key_row, value_row, seg_key = inputs
        scores, allowed = row_scores(query_row, seg_query, key_row, seg_key)
        probs = jnp.where(allowed, jnp.exp(scores - lse_row[:, :, None]), 0.0)
        grad_probs = jnp.einsum(
            "qhe,khe->hqk", heads_row, value_row, preferred_element_type=jnp.float32
        )
        grad_scores = (probs * (grad_probs - delta_row[:, :, None])).astype(bfloat)
        query_part = (
            jnp.einsum("hqk,khe->qhe", grad_scores, key_row, preferred_element_type=jnp.float32)
            * scale
        )
        key_part = (
            jnp.einsum("hqk,qhe->khe", grad_scores, query_row, preferred_element_type=jnp.float32)
            * scale
        )
        value_part = jnp.einsum(
            "hqk,qhe->khe", probs.astype(bfloat), heads_row, preferred_element_type=jnp.float32
        )
        return (
            query_part,
            jnp.concatenate(
                [key_part.reshape(count, local_width), value_part.reshape(count, local_width)],
                axis=1,
            ),
        )

    query_parts, pair_parts = lax.map(
        back_one_row,
        (query, seg_all, log_total, delta, grad_heads, key_piece, value_piece, seg_piece),
    )
    own_pairs = lax.psum_scatter(
        pair_parts.astype(jnp.bfloat16), "seq", scatter_dimension=1, tiled=True
    ).astype(jnp.float32)
    grad_proj = jnp.concatenate(
        [query_parts.reshape(rows_here, section, local_width), own_pairs], axis=2
    ).astype(bfloat)
    grad_normed = lax.psum_scatter(
        jnp.einsum(
            "rlw,dw->rld", grad_proj, proj_weight, preferred_element_type=jnp.float32
        ).astype(jnp.bfloat16),
        "mp",
        scatter_dimension=1,
        tiled=True,
    ).astype(jnp.float32)
    proj_grads = tokens_dot(normed_all, grad_proj)
    bias_sums = jnp.sum(grad_proj, axis=(0, 1), dtype=jnp.float32)
    bias_pair = jnp.concatenate([bias_sums[:local_width], bias_sums[2 * local_width :]])
    unused, first_back = jax.vjp(layer_norm, hidden, first_gain, first_shift)
    grad_hidden, grad_gain_first, grad_shift_first = first_back(grad_normed)
    token_grad = grad_residual + grad_hidden
    table_grad = jnp.einsum("rt,rd->td", picks, jnp.sum(token_grad, axis=1), precision=highest)
    out_bias_term = jnp.sum(grad_residual, axis=(0, 1))
    down_bias_term = jnp.sum(cotangent, axis=(0, 1), dtype=jnp.float32)
    head_total = lax.psum(
        (proj_grads, bias_pair, grad_out, unit_grads[0], unit_grads[1], unit_grads[2]),
        ("dp", "seq"),
    )
    common_total = lax.psum(
        (
            table_grad,
            grad_gain_first,
            grad_shift_first,
            out_bias_term,
            grad_gain_second,
            grad_shift_second,
            down_bias_term,
        ),
        ("dp", "seq", "mp"),
    )
    up_grad, up_bias_grad, down_grad = (head_total[3], head_total[4], head_total[5])
    proj_total = head_total[0]
    return (
        result,
        token_grad,
        common_total[0],
        common_total[1],
        common_total[2],
        proj_total[:, :local_width],
        head_total[1][:local_width],
        proj_total[:, local_width : 2 * local_width],
        proj_total[:, 2 * local_width :],
        head_total[1][local_width:],
        head_total[2],
        common_total[3],
        common_total[4],
        common_total[5],
        up_grad,
        up_bias_grad,
        down_grad,
        common_total[6],
    )


def solution(mesh):
    in_specs = (
        P("dp", ("seq", "mp"), None),
        P("dp", ("seq", "mp")),
        P("dp"),
        P(),
        P(),
        P(),
        P(None, "mp"),
        P("mp"),
        P(None, "mp"),
        P(None, "mp"),
        P("mp"),
        P("mp", None),
        P(),
        P(),
        P(),
        P(None, "mp"),
        P("mp"),
        P("mp", None),
        P(),
        P("dp", ("seq", "mp"), None),
    )
    out_specs = (
        P("dp", ("seq", "mp"), None),
        P("dp", ("seq", "mp"), None),
        P(),
        P(),
        P(),
        P(None, "mp"),
        P("mp"),
        P(None, "mp"),
        P(None, "mp"),
        P("mp"),
        P("mp", None),
        P(),
        P(),
        P(),
        P(None, "mp"),
        P("mp"),
        P("mp", None),
        P(),
    )
    return jax.shard_map(local, mesh=mesh, in_specs=in_specs, out_specs=out_specs, check_vma=False)
```

profile of v0, /device:TPU:0, one launch (start us, length us, event | category | flops | bytes accessed | tf_op | source)
XLA Modules:
  0.0 712.8 jit_solution(10863600706411942458)
XLA Ops:
  7.3 1.6 fusion.95
  10.0 1.1 multiply_reduce_fusion.2
  12.9 2.3 all_gather.29
  18.4 1.8 all_gather.27
  20.3 22.1 %all_gather.28 = bf16[2,2048]{1,0:T(2,128)(2,1)S(1)} all-gather(bf16[2,256]{1,0:T(2,128)(2,1)S(1)} %all_gather.27), channel_id=1, replica_groups=mesh['dp'=2,'seq'=8,'mp'=2] {'seq'}, dimensions={1}, use_global_device_ids=true | all-gather | bytes 9216 | tf_op jit(solution)/shard_map/all_gather | solution.py:104
  42.4 26.4 %all-gather.3.cloned.1.call-done = bf16[2,2048,256]{2,1,0:T(8,128)(2,1)} async-done(((bf16[2,256,256]{2,1,0:T(8,128)(2,1)}), bf16[2,2048,256]{2,1,0:T(8,128)(2,1)}) %all-gather.3.cloned.1.call-update) | async-done | bytes 2097168 | tf_op jit(solution)/shard_map/all_gather | solution.py:102
  68.8 3.9 copy.51
  72.7 46.6 %all-gather.5.cloned.1.call-done = bf16[2,2048,256]{2,1,0:T(8,128)(2,1)} async-done(((bf16[2,256,256]{2,1,0:T(8,128)(2,1)}), bf16[2,2048,256]{2,1,0:T(8,128)(2,1)}) %all-gather.5.cloned.1.call-update) | async-done | bytes 2097168 | tf_op jit(solution)/shard_map/all_gather | solution.py:103
  119.4 3.9 copy.52
  123.3 19.1 %while.28 = (s32[]{:T(128)}, f32[2,4,256]{2,1,0:T(4,128)S(1)}, f32[2,4,256]{2,1,0:T(4,128)S(1)}, f32[2,256,4,64]{1,3,2,0:T(8,128)S(1)}, bf16[2,256]{1,0:T(2,128)...) while((s32[]{:T(128)}, f32[2,4,256]{2,1,0:T(4,128)S(1)}, ...), condition=%wide.region_5.6_spmd.clone, body=%wide.region_2.5_spmd.sunk.clone | while | flops 564728832 | bytes 29818480 | solution.py:120
  123.7 3.1 fusion.171
  126.8 2.5 fusion.172
  129.4 3.5 fusion.174
  133.3 3.1 fusion.171
  136.4 2.5 fusion.172
  138.9 3.5 fusion.174
  143.8 2.4 all_gather.33
  146.3 4.0 reduce-scatter.6.cloned.1.call-done
  151.4 1.2 multiply_reduce_fusion.1
  153.8 2.5 all_gather.32
  157.8 1.9 convert_reduce_fusion
  160.7 1.5 convolution_convert_fusion.2
  163.1 8.5 %reduce-scatter.10.cloned.1.call-done = bf16[2,128,512]{2,1,0:T(8,128)(2,1)} async-done(((bf16[2,256,512]{2,1,0:T(8,128)(2,1)}), bf16[2,128,512]{2,1,0:T(8,128)(2,1)}) %reduce-scatter.10.cloned.1.call-update) | async-done | bytes 262160 | tf_op jit(solution)/shard_map/reduce_scatter | solution.py:162
  171.6 1.2 convert_reduce_fusion.3
  172.8 1.3 fusion.92
  174.1 1.2 fusion.104
  175.3 2.2 all_gather.34
  179.4 44.1 %while.29 = (s32[]{:T(128)}, bf16[2,256,4,64]{1,3,2,0:T(8,128)(2,1)}, bf16[2,2048,512]{2,1,0:T(8,128)(2,1)}, bf16[2,2048,4,64]{1,3,2,0:T(8,128)(2,1)}, bf16[2,25...) while((s32[]{:T(128)}, ...), condition=%wide.region_15.16_spmd.clone, body=%wide.region_14.15_spmd.sunk.clone | while | flops 1373175808 | bytes 57979532 | solution.py:223
  179.4 2.6 fusion.185
  182.4 4.8 multiply_convert_fusion.6
  187.2 3.3 fusion.187
  190.5 3.4 fusion.188
  193.8 1.8 convolution_multiply_fusion.4
  195.6 1.5 maximum_bitcast_fusion.6
  197.1 2.9 copy.85
  200.0 1.5 constant_dynamic-update-slice_fusion.3
  201.5 2.6 fusion.185
  204.5 4.8 multiply_convert_fusion.6
  209.3 3.3 fusion.187
  212.6 3.4 fusion.188
  215.9 1.8 convolution_multiply_fusion.4
  217.7 1.5 maximum_bitcast_fusion.6
  219.2 2.9 copy.85
  222.1 1.4 constant_dynamic-update-slice_fusion.3
  223.6 1.5 copy-done.15
  225.1 1.7 convolution_convert_fusion.3
  228.0 84.9 %reduce-scatter.12.cloned.1.call-done = bf16[2,256,512]{2,1,0:T(8,128)(2,1)} async-done(((bf16[2,2048,512]{2,1,0:T(8,128)(2,1)}), bf16[2,256,512]{2,1,0:T(8,128)(2,1)}) %reduce-scatter.12.cloned.1.call-update) | async-done | bytes 524304 | tf_op jit(solution)/shard_map/reduce_scatter | solution.py:227
  312.9 2.7 convolution_convert_fusion
  315.9 2.0 convolution_bitcast_fusion.1
  318.0 2.4 convolution_bitcast_fusion
  321.5 1.8 convolution_bitcast_fusion.2
  324.0 11.4 %reduce-scatter.14.cloned.1.call-done = bf16[2,128,512]{2,1,0:T(8,128)(2,1)} async-done(((bf16[2,256,512]{2,1,0:T(8,128)(2,1)}), bf16[2,128,512]{2,1,0:T(8,128)(2,1)}) %reduce-scatter.14.cloned.1.call-update) | async-done | bytes 262160 | tf_op jit(solution)/shard_map/reduce_scatter | solution.py:233
  335.4 2.4 fusion.83
  337.8 1.3 fusion.84
  339.1 1.3 fusion.105
  340.4 2.4 fusion.93
  343.0 45.4 %all-reduce.1 = (f32[512]{0:T(512)S(1)}, f32[1024]{0:T(1024)}) all-reduce(f32[512]{0:T(512)S(1)} %pad_maximum_fusion.3, f32[1024]{0:T(1024)S(1)} %get-tuple-element.236), channel_id=1, replica_groups=mesh['dp'=2,'seq'=8,'mp'=2] {'dp','seq'}, use_global_device_ids=true, to_apply=%region_28.29 | all-reduce | flops 1536 | bytes 12288 | tf_op jit(solution)/shard_map/psum | solution.py:250
  389.0 38.0 %all-reduce = (f32[512]{0:T(512)}, f32[512]{0:T(512)}, f32[512]{0:T(512)}, f32[512]{0:T(512)}, f32[512]{0:T(512)}, /*index=5*/f32[512]{0:T(512)}) all-reduce(f32[512]{0:T(512)S(1)} %get-tuple-element.152, f32[512]{0:T(512)S(1)} %get-tuple-element.155, ...), channel_id=1, replica_groups=mesh['dp'=2,'seq'=8,'mp'=2] {'dp','seq','mp'}, use_global_device_ids=true, to_apply=%region_23.24 | all-reduce | flops 3072 | bytes 24576 | tf_op jit(solution)/shard_map/psum | solution.py:254
  427.0 132.6 %all-reduce.8.cloned.1.call-done = (f32[512,768]{1,0:T(8,128)}, f32[256,512]{1,0:T(8,128)}, f32[512,1024]{1,0:T(8,128)}, f32[1024,512]{1,0:T(8,128)}) async-done(((f32[512,768]{1,0:T(8,128)}, f32[256,512]{1,0:T(8,128)}, f32[512,1024]{1,0:T(8,128)}, f32[1024,512]{1,0:T(8,128)}), (f32[512,768]{1,0:T(8,128)}, f32[256,512]{1,0:T(8,128)}, f32[512,1024]{1,0:T(8,128)}, ...) | async-done | bytes 6291472 | tf_op jit(solution)/shard_map/psum | solution.py:250
  559.5 2.5 fusion.106
  562.0 136.6 %all-reduce.6.cloned.1.call-done = f32[1000,512]{1,0:T(8,128)} async-done(((f32[1000,512]{1,0:T(8,128)}), f32[1000,512]{1,0:T(8,128)}) %all-reduce.6.cloned.1.call-update) | async-done | bytes 2048016 | tf_op jit(solution)/shard_map/psum | solution.py:254
  698.6 3.2 copy.119
  702.6 1.3 copy.121
  705.0 1.3 copy.122
  (174 shorter events, 22.4 us)
Async XLA Ops:
  7.2 150.6 %copy-start = (bf16[1024,512]{1,0:T(8,128)(2,1)S(1)}, bf16[1024,512]{1,0:T(8,128)(2,1)}, u32[]{:S(2)}) copy-start(bf16[1024,512]{1,0:T(8,128)(2,1)} %param.41) | copy-start | bytes 3145732
  7.2 8.0 %copy-start.43 = (bf16[256]{0:T(256)(128)(2,1)S(1)}, bf16[256]{0:T(256)(128)(2,1)}, u32[]{:S(2)}) copy-start(bf16[256]{0:T(256)(128)(2,1)} %param.34) | copy-start | bytes 1540
  7.2 8.0 %copy-start.44 = (bf16[256]{0:T(256)(128)(2,1)S(1)}, bf16[256]{0:T(256)(128)(2,1)}, u32[]{:S(2)}) copy-start(bf16[256]{0:T(256)(128)(2,1)} %param.31) | copy-start | bytes 1540
  7.2 8.0 %copy-start.45 = (bf16[512,256]{1,0:T(8,128)(2,1)S(1)}, bf16[512,256]{1,0:T(8,128)(2,1)}, u32[]{:S(2)}) copy-start(bf16[512,256]{1,0:T(8,128)(2,1)} %param.33) | copy-start | bytes 786436
  7.2 8.0 %copy-start.46 = (bf16[512,256]{1,0:T(8,128)(2,1)S(1)}, bf16[512,256]{1,0:T(8,128)(2,1)}, u32[]{:S(2)}) copy-start(bf16[512,256]{1,0:T(8,128)(2,1)} %param.32) | copy-start | bytes 786436
  7.2 8.0 %copy-start.47 = (bf16[512,256]{1,0:T(8,128)(2,1)S(1)}, bf16[512,256]{1,0:T(8,128)(2,1)}, u32[]{:S(2)}) copy-start(bf16[512,256]{1,0:T(8,128)(2,1)} %param.30) | copy-start | bytes 786436
  7.3 61.5 %all-gather.3.cloned.1.call-start = ((), (), s32[]{:S(2)}) async-start(), calls=%async_computation.5 | async-start | bytes 2359296 | tf_op jit(solution)/shard_map/all_gather | solution.py:102
  10.0 5.2 copy-start.31
  11.2 0.6 copy-start.36
  11.8 3.4 copy-start.34
  15.2 1.6 copy-start.19
  15.3 2.3 copy-start.48
  16.8 102.6 %all-gather.5.cloned.1.call-start = ((), (), s32[]{:S(2)}) async-start(), calls=%async_computation.6 | async-start | bytes 2359296 | tf_op jit(solution)/shard_map/all_gather | solution.py:103
  17.5 132.8 %reduce-scatter.6.cloned.1.call-start = ((), (), s32[]{:S(2)}) async-start(), calls=%async_computation.7 | async-start | bytes 786432 | tf_op jit(solution)/shard_map/reduce_scatter | solution.py:139
  123.3 19.3 %copy-start.25 = (bf16[256,512]{1,0:T(8,128)(2,1)S(1)}, bf16[256,512]{1,0:T(8,128)(2,1)}, u32[]{:S(2)}) copy-start(bf16[256,512]{1,0:T(8,128)(2,1)} %param.35) | copy-start | bytes 786436
  142.4 1.4 copy-start.41
  142.4 1.4 copy-start.40
  142.4 1.4 copy-start.9
  142.4 7.9 %copy-start.1 = (bf16[2,128,512]{2,1,0:T(8,128)(2,1)S(1)}, bf16[2,128,512]{2,1,0:T(8,128)(2,1)}, u32[]{:S(2)}) copy-start(bf16[2,128,512]{2,1,0:T(8,128)(2,1)} %param.24) | copy-start | bytes 786436
  142.5 10.2 %copy-start.30 = (f32[512]{0:T(512)S(1)}, f32[512]{0:T(512)}, u32[]{:S(2)}) copy-start(f32[512]{0:T(512)} %param.37) | copy-start | bytes 6148
  142.5 10.2 %copy-start.39 = (f32[512]{0:T(512)S(1)}, f32[512]{0:T(512)}, u32[]{:S(2)}) copy-start(f32[512]{0:T(512)} %param.38) | copy-start | bytes 6148
  142.6 11.2 %copy-start.11 = (bf16[2,256,256]{1,2,0:T(8,128)(2,1)}, bf16[2,256,256]{1,2,0:T(8,128)(2,1)S(1)}, u32[]{:S(2)}) copy-start(bf16[2,256,256]{1,2,0:T(8,128)(2,1)S(1)} %fusion.85) | copy-start | bytes 786436
  143.7 13.4 %copy-start.22 = (bf16[512,1024]{1,0:T(8,128)(2,1)S(1)}, bf16[512,1024]{1,0:T(8,128)(2,1)}, u32[]{:S(2)}) copy-start(bf16[512,1024]{1,0:T(8,128)(2,1)} %param.39) | copy-start | bytes 3145732
  143.7 27.9 %reduce-scatter.10.cloned.1.call-start = ((), (), s32[]{:S(2)}) async-start(), calls=%async_computation.9 | async-start | bytes 786432 | tf_op jit(solution)/shard_map/reduce_scatter | solution.py:162
  153.8 4.0 copy-start.27
  156.3 0.8 copy-start.5
  157.8 1.9 copy-start.14
  159.8 1.0 copy-start.23
  160.7 10.8 %copy-start.2 = (bf16[2,128,512]{2,1,0:T(8,128)(2,1)S(1)}, bf16[2,128,512]{2,1,0:T(8,128)(2,1)}, u32[]{:S(2)}) copy-start(bf16[2,128,512]{2,1,0:T(8,128)(2,1)} %reduce-scatter.6.cloned.1.call-done) | copy-start | bytes 786436
  162.3 16.0 %copy-start.26 = (bf16[256,512]{1,0:T(8,128)(2,1)S(1)}, bf16[256,512]{1,0:T(8,128)(2,1)}, u32[]{:S(2)}) copy-start(bf16[256,512]{1,0:T(8,128)(2,1)} %param.35) | copy-start | bytes 786436
  162.3 150.6 %reduce-scatter.12.cloned.1.call-start = ((), (), s32[]{:S(2)}) async-start(), calls=%async_computation.10 | async-start | bytes 4718592 | tf_op jit(solution)/shard_map/reduce_scatter | solution.py:227
  177.5 0.8 copy-start.7
  223.5 1.6 copy-start.15
  223.5 100.4 %reduce-scatter.8.cloned.1.call-start = ((), (), s32[]{:S(2)}) async-start(), calls=%async_computation.8 | async-start | bytes 786432 | tf_op jit(solution)/shard_map/reduce_scatter | solution.py:151
  226.8 108.6 %reduce-scatter.14.cloned.1.call-start = ((), (), s32[]{:S(2)}) async-start(), calls=%async_computation.11 | async-start | bytes 786432 | tf_op jit(solution)/shard_map/reduce_scatter | solution.py:233
  228.0 87.9 %copy-start.6 = (bf16[2,256,512]{2,1,0:T(8,128)(2,1)S(1)}, bf16[2,256,512]{2,1,0:T(8,128)(2,1)}, u32[]{:S(2)}) copy-start(bf16[2,256,512]{2,1,0:T(8,128)(2,1)} %copy-done.5) | copy-start | bytes 1572868
  228.0 87.9 %copy-start.24 = (bf16[2,256,1024]{2,1,0:T(8,128)(2,1)S(1)}, bf16[2,256,1024]{2,1,0:T(8,128)(2,1)}, u32[]{:S(2)}) copy-start(bf16[2,256,1024]{2,1,0:T(8,128)(2,1)} %copy-done.23) | copy-start | bytes 3145732
  315.6 243.9 %all-reduce.8.cloned.1.call-start = ((), (), s32[]{:S(2)}) async-start(), calls=%async_computation.13 | async-start | bytes 12582912 | tf_op jit(solution)/shard_map/psum | solution.py:250
  315.9 2.1 copy-start.16
  315.9 2.1 copy-start.28
  318.0 2.4 copy-start.8
  318.0 2.4 copy-start.12
  318.0 3.5 copy-start.20
  318.0 3.5 copy-start.21
  323.3 0.7 copy-start.42
  323.3 12.1 %copy-start.3 = (bf16[2,128,512]{2,1,0:T(8,128)(2,1)S(1)}, bf16[2,128,512]{2,1,0:T(8,128)(2,1)}, u32[]{:S(2)}) copy-start(bf16[2,128,512]{2,1,0:T(8,128)(2,1)} %reduce-scatter.6.cloned.1.call-done) | copy-start | bytes 786436
  323.3 12.1 %copy-start.4 = (bf16[2,128,512]{2,1,0:T(8,128)(2,1)S(1)}, bf16[2,128,512]{2,1,0:T(8,128)(2,1)}, u32[]{:S(2)}) copy-start(bf16[2,128,512]{2,1,0:T(8,128)(2,1)} %reduce-scatter.10.cloned.1.call-done) | copy-start | bytes 786436
  323.3 12.1 %copy-start.10 = (bf16[2,128,512]{2,1,0:T(8,128)(2,1)S(1)}, bf16[2,128,512]{2,1,0:T(8,128)(2,1)}, u32[]{:S(2)}) copy-start(bf16[2,128,512]{2,1,0:T(8,128)(2,1)} %param.43) | copy-start | bytes 786436
  323.3 12.1 %copy-start.32 = (f32[2,128]{1,0:T(2,128)S(1)}, f32[2,128]{1,0:T(2,128)}, u32[]{:S(2)}) copy-start(f32[2,128]{1,0:T(2,128)} %copy-done.31) | copy-start | bytes 3076
  323.3 12.1 %copy-start.33 = (f32[512]{0:T(512)S(1)}, f32[512]{0:T(512)}, u32[]{:S(2)}) copy-start(f32[512]{0:T(512)} %param.28) | copy-start | bytes 6148
  323.3 14.5 %copy-start.37 = (f32[2,128]{1,0:T(2,128)S(1)}, f32[2,128]{1,0:T(2,128)}, u32[]{:S(2)}) copy-start(f32[2,128]{1,0:T(2,128)} %copy-done.36) | copy-start | bytes 3076
  323.3 14.5 %copy-start.35 = (f32[2,128]{1,0:T(2,128)S(1)}, f32[2,128]{1,0:T(2,128)}, u32[]{:S(2)}) copy-start(f32[2,128]{1,0:T(2,128)} %copy-done.34) | copy-start | bytes 3076
  323.4 375.3 %all-reduce.6.cloned.1.call-start = ((), (), s32[]{:S(2)}) async-start(), calls=%async_computation.12 | async-start | bytes 4096000 | tf_op jit(solution)/shard_map/psum | solution.py:254
  324.0 16.5 %copy-start.38 = (s32[2]{0:T(128)S(1)}, s32[2]{0:T(128)}, u32[]{:S(2)}) copy-start(s32[2]{0:T(128)} %param.26) | copy-start | bytes 28
  335.4 3.7 copy-start.13
  562.0 139.8 %copy-start.29 = (f32[256,512]{1,0:T(8,128)S(1)}, f32[256,512]{1,0:T(8,128)}, u32[]{:S(2)}) copy-start(f32[256,512]{1,0:T(8,128)} %get-tuple-element.498) | copy-start | bytes 1572868
  698.6 4.0 copy-start.18
  702.6 2.3 copy-start.17
Sparse Core Ops, SparseCore 0:
  16.9 51.8 all-gather.2
  71.6 47.7 all-gather.4
  143.8 6.4 reduce-scatter.5
  162.4 9.1 reduce-scatter.9
  223.6 89.2 reduce-scatter.11
  315.7 7.6 reduce-scatter.7
  326.2 9.1 reduce-scatter.13
  344.1 215.3 all-reduce.7
  566.3 132.3 all-reduce.5
where the time goes:
time: 714 us; the launch traced here: 713 us
  waiting for transfers between devices  452 us (63%)
  blocking collectives  117 us (16%)
  matrix products  67.2 us (9%)
  local copies, waits for them, and re-layouts  35.7 us (5%)
  other arithmetic  26.1 us (4%)
  between operations  14.5 us (2%)
    psum x1, waiting for transfers between devices, local(): lax.psum((table_grad, grad_gain_first, grad_shift_first, out_bias_term, g...  137 us
    psum x1, waiting for transfers between devices, local(): lax.psum((proj_grads, bias_pair, grad_out, unit_grads[0], unit_grads[1],...  133 us
    reduce_scatter x1, waiting for transfers between devices, local(): lax.psum_scatter(pair_parts.astype(jnp.bfloat16), 'seq', scatter_dimensio...  84.9 us
    all_gather x1, waiting for transfers between devices, local(): lax.all_gather(values, 'seq', axis=1, tiled=True)  46.6 us
    psum x1, blocking collectives, local(): lax.psum((proj_grads, bias_pair, grad_out, unit_grads[0], unit_grads[1],...  45.4 us
    psum x1, blocking collectives, local(): lax.psum((table_grad, grad_gain_first, grad_shift_first, out_bias_term, g...  38 us
    all_gather x1, waiting for transfers between devices, local(): lax.all_gather(keys, 'seq', axis=1, tiled=True)  26.4 us
    all_gather x1, blocking collectives, local(): lax.all_gather(seg_all, 'seq', axis=1, tiled=True)  22.1 us
  transfers between devices with their start and end apart: 9, of which 8 were waited for; matrix products, arithmetic and copies ran while one was open for 4% of the time, Pallas kernels for 0%

commit v1 on v0

v1 whole, which is shorter than its diff:
```python
import functools
import math

import jax
import jax.numpy as jnp
from jax import lax
from jax.experimental import pallas as pl
from jax.experimental.pallas import tpu as pltpu
from jax.sharding import PartitionSpec as P

MESH = pl.DeviceIdType.MESH
BF, F32 = jnp.bfloat16, jnp.float32
NN = (((1,), (0,)), ((), ()))
NT = (((1,), (1,)), ((), ()))
TN = (((0,), (0,)), ((), ()))
HEAD_DIM = 64
BLOCK = 128
PAIR = 2 * HEAD_DIM
MASKED = -1e30
GELU_A = 0.044715
GELU_C = math.sqrt(2.0 / math.pi)
UP_AT, DOWN_AT, OUT_AT, Q_AT, K_AT, V_AT, WG_ROWS = 0, 2048, 4096, 4608, 5120, 5632, 6144
SV_TABLE = 16


def dot(a, b, dims):
    return lax.dot_general(a, b, dims, preferred_element_type=F32)


def bit(v, n):
    return lax.rem(lax.div(v, n), 2)


def flip(v, n):
    return v + n - 2 * n * bit(v, n)


def here():
    return lax.axis_index("dp"), lax.axis_index("seq"), lax.axis_index("mp")


def neighbour(name):
    dp, seq, mp = here()
    if name == "core":
        return (dp, seq, 1 - mp)
    if name == "x":
        return (1 - dp, seq, mp)
    if name == "y":
        return (dp, flip(seq, 1), mp)
    if name == "zl":
        return (dp, flip(seq, 2), mp)
    if name == "diag":
        return (dp, flip(flip(seq, 1), 2), mp)
    return (dp, flip(seq, 4), mp)


def side(name):
    dp, seq, mp = here()
    return {"x": dp, "y": bit(seq, 1), "zl": bit(seq, 2), "zh": bit(seq, 4), "core": mp}[name]


def greet(names):
    barrier = pltpu.get_barrier_semaphore()
    for name in names:
        pl.semaphore_signal(barrier, inc=1, device_id=neighbour(name), device_id_type=MESH)
    pl.semaphore_wait(barrier, len(names))


class Wire:
    def __init__(self, send_sem, recv_sem):
        self.send_sem, self.recv_sem = send_sem, recv_sem
        self.sent = []

    def send(self, src, dst, name):
        n = len(self.sent)
        copy = pltpu.make_async_remote_copy(
            src_ref=src,
            dst_ref=dst,
            send_sem=self.send_sem.at[n],
            recv_sem=self.recv_sem.at[n],
            device_id=neighbour(name),
            device_id_type=MESH,
        )
        copy.start()
        self.sent.append(copy)
        return copy

    def finish(self):
        for copy in self.sent:
            copy.wait_send()


PEERS = ("y", "zl", "diag")
GATHER_COPIES = 48


def gather_kernel(
    tokens, cot, segs, wq, wk, wv, wo, up, down, bias,
    xrow, seg_all, cot2, wq_f, wk_f, wv_f, wo_f, up_f, down_f, bias_f,
    send_sem, recv_sem, local_sem,
):
    dp, seq, mp = here()
    g = lax.div(seq, 4)
    own = 2 * seq + mp
    par = 2 * flip(seq, 4) + mp
    greet(("core", "zh") + PEERS)
    wire = Wire(send_sem, recv_sem)
    locals_ = []

    def keep(src, dst):
        copy = pltpu.make_async_copy(src, dst, local_sem.at[len(locals_)])
        copy.start()
        locals_.append(copy)

    def columns(ref):
        w = ref.shape[1] // 2
        return ref.at[:, pl.ds(pl.multiple_of(mp * w, w), w)]

    def rows(ref):
        w = ref.shape[0] // 2
        return ref.at[pl.ds(pl.multiple_of(mp * w, w), w)]

    crossing = [
        wire.send(tokens.at[1 - g], xrow.at[own], "zh"),
        wire.send(segs.at[1 - g], seg_all.at[own], "zh"),
    ]
    cot_copy = wire.send(cot.at[1 - g], cot2.at[1], "zh")
    first = []
    for name in PEERS:
        first.append(wire.send(tokens.at[g], xrow.at[own], name))
        first.append(wire.send(segs.at[g], seg_all.at[own], name))
    last = [
        wire.send(tokens.at[g], xrow.at[own], "core"),
        wire.send(segs.at[g], seg_all.at[own], "core"),
    ]
    for src, dst in (
        (wk, columns(wk_f)), (wv, columns(wv_f)), (wq, columns(wq_f)), (bias, bias_f.at[mp]),
        (wo, rows(wo_f)), (up, columns(up_f)), (down, rows(down_f)),
    ):
        last.append(wire.send(src, dst, "core"))
        keep(src, dst)
    keep(tokens.at[g], xrow.at[own])
    keep(segs.at[g], seg_all.at[own])
    keep(cot.at[g], cot2.at[0])
    for copy in crossing:
        copy.wait_recv()
    second = []
    for name in PEERS:
        second.append(wire.send(xrow.at[par], xrow.at[par], name))
        second.append(wire.send(seg_all.at[par], seg_all.at[par], name))
    last.append(wire.send(xrow.at[par], xrow.at[par], "core"))
    last.append(wire.send(seg_all.at[par], seg_all.at[par], "core"))
    for copies, base in ((first, seq), (second, flip(seq, 4))):
        for i, name in enumerate(PEERS):
            copies[2 * i].wait_recv()
            copies[2 * i + 1].wait_recv()
            there = {"y": flip(base, 1), "zl": flip(base, 2), "diag": flip(flip(base, 1), 2)}[name]
            block = 2 * there + mp
            last.append(wire.send(xrow.at[block], xrow.at[block], "core"))
            last.append(wire.send(seg_all.at[block], seg_all.at[block], "core"))
    for copy in locals_:
        copy.wait()
    cot_copy.wait_recv()
    for copy in last:
        copy.wait_recv()
    wire.finish()


def any_spec(n):
    return [pl.BlockSpec(memory_space=pl.ANY)] * n


def vmem_spec(n):
    return [pl.BlockSpec(memory_space=pltpu.VMEM)] * n


def gather(tokens, cot, segs, wq, wk, wv, wo, up, down, bias):
    shape = jax.ShapeDtypeStruct
    d = tokens.shape[2]
    blocks = 2 * lax.axis_size("seq")
    return pl.pallas_call(
        gather_kernel,
        out_shape=(
            shape((blocks, BLOCK, d), BF),
            shape((blocks, 8, BLOCK), F32),
            shape(cot.shape, BF),
            shape((d, 2 * wq.shape[1]), BF),
            shape((d, 2 * wk.shape[1]), BF),
            shape((d, 2 * wv.shape[1]), BF),
            shape((2 * wo.shape[0], d), BF),
            shape((d, 2 * up.shape[1]), BF),
            shape((2 * down.shape[0], d), BF),
            shape((2,) + bias.shape, F32),
        ),
        in_specs=any_spec(10),
        out_specs=tuple(any_spec(10)),
        scratch_shapes=[
            pltpu.SemaphoreType.DMA((GATHER_COPIES,)),
            pltpu.SemaphoreType.DMA((GATHER_COPIES,)),
            pltpu.SemaphoreType.DMA((10,)),
        ],
        compiler_params=pltpu.CompilerParams(collective_id=0, has_side_effects=True),
        name="gather",
    )(tokens, cot, segs, wq, wk, wv, wo, up, down, bias)


def normalise(value):
    centred = value - jnp.mean(value, axis=-1, keepdims=True)
    rstd = lax.rsqrt(jnp.mean(centred * centred, axis=-1, keepdims=True) + 1e-5)
    return centred * rstd, rstd


def normalise_back(grad_hat, hat, rstd):
    return rstd * (
        grad_hat
        - jnp.mean(grad_hat, axis=-1, keepdims=True)
        - hat * jnp.mean(grad_hat * hat, axis=-1, keepdims=True)
    )


def column_sum(value):
    return jnp.sum(value, axis=0, keepdims=True)


def layer_kernel(
    xrow, seg_all, cot2, embed, vecs, wq, wk, wv, wo, up, down, bias, ids,
    result2, wg, sv, t_out,
    normed, k_ref, v_ref, hot, s_buf, att, att_t, lse, q_ref, dk_ref, dv_ref, dq_ref, t_buf, dwk, dwv,
):
    dp, seq, mp = here()
    own = 2 * seq + mp
    par = 2 * flip(seq, 4) + mp
    d = normed.shape[1]
    length = normed.shape[0]
    pairs = d // PAIR
    step = 512
    steps = length // step
    nb = step // BLOCK
    ff = up.shape[1]
    row_embed = embed[...]
    gain, shift = vecs[0:1, :], vecs[1:2, :]

    def bias_row(r, n):
        return jnp.concatenate([bias[m, r + i : r + i + 1, :] for m in range(2) for i in range(n)], axis=1)

    value_bias = bias_row(1, 1)

    def hidden_of(block):
        return block.astype(F32) + row_embed

    def seg_column(block):
        return jnp.transpose(block)[:, 0:1]

    def project(c, carry):
        at = pl.ds(pl.multiple_of(c * step, step), step)
        hat, _ = normalise(hidden_of(xrow[pl.ds(c * nb, nb)].reshape(step, d)))
        low = (hat * gain + shift).astype(BF)
        normed[at, :] = low
        k_ref[at, :] = dot(low, wk[...], NN).astype(BF)
        v_ref[at, :] = (dot(low, wv[...], NN) + value_bias).astype(BF)
        spans = jnp.concatenate([seg_column(seg_all[c * nb + i]) for i in range(nb)], axis=0)
        lanes = lax.broadcasted_iota(jnp.int32, (step, BLOCK), 1).astype(F32)
        hot[at, :] = jnp.where(spans == lanes, 1.0, 0.0).astype(BF)
        return carry

    lax.fori_loop(0, steps, project, 0)

    def query_rows(ref):
        return jnp.concatenate(
            [ref[pl.ds(pl.multiple_of(b * BLOCK, BLOCK), BLOCK), :] for b in (own, par)], axis=0
        )

    normed_q = query_rows(normed)
    q_ref[...] = ((dot(normed_q, wq[...], NN) + bias_row(0, 1)).astype(BF).astype(F32) * (1.0 / math.sqrt(HEAD_DIM))).astype(BF)
    spans_q = jnp.concatenate([seg_column(seg_all[own]), seg_column(seg_all[par])], axis=0)
    nq = 2 * BLOCK
    lanes_q = lax.broadcasted_iota(jnp.int32, (nq, BLOCK), 1).astype(F32)
    other = jnp.where(spans_q == lanes_q, 0.0, MASKED).astype(BF)
    live = jnp.where(spans_q > 0.0, 1.0, 0.0)
    other2 = jnp.concatenate([other, other], axis=0)
    first_head = lax.broadcasted_iota(jnp.int32, (nq, PAIR), 1) < HEAD_DIM
    first_head_t = lax.broadcasted_iota(jnp.int32, (PAIR, nq), 0) < HEAD_DIM

    def split_heads(value):
        wide = value.astype(F32)
        return jnp.concatenate(
            [jnp.where(first_head, wide, 0.0), jnp.where(first_head, 0.0, wide)], axis=0
        ).astype(BF)

    def join_heads_t(value):
        return jnp.where(first_head_t, value[:, :nq], value[:, nq:])

    def lanes_of(p):
        return pl.ds(pl.multiple_of(p * PAIR, PAIR), PAIR)

    def chunk(c):
        return pl.ds(c * step, step)

    def attend(p, carry):
        at = lanes_of(p)
        query = jnp.concatenate([split_heads(q_ref[:, at]), other2], axis=1)
        top = jnp.full((8, 2 * nq), -3e38, F32)
        for c in range(steps):
            keys = jnp.concatenate([k_ref[chunk(c), at], hot[chunk(c), :]], axis=1)
            scores = dot(keys, query, NT)
            s_buf[chunk(c), :] = scores
            top = jnp.maximum(top, jnp.max(scores.reshape(step // 8, 8, 2 * nq), axis=0))
        top = jnp.max(top, axis=0, keepdims=True)
        total = jnp.zeros((8, 2 * nq), F32)
        summed = jnp.zeros((PAIR, 2 * nq), F32)
        for c in range(steps):
            weights = jnp.exp(s_buf[chunk(c), :] - top)
            total = total + jnp.sum(weights.reshape(step // 8, 8, 2 * nq), axis=0)
            summed = summed + dot(v_ref[chunk(c), at], weights.astype(BF), TN)
        total = jnp.sum(total, axis=0, keepdims=True)
        joined = join_heads_t(summed / total)
        att_t[p] = joined
        att[:, at] = jnp.transpose(joined)
        lse[p] = jnp.broadcast_to(top + jnp.log(total), (8, 2 * nq))
        return carry

    lax.fori_loop(0, pairs, attend, 0)

    mixed = (att[...] * live).astype(BF)
    hidden_q = hidden_of(jnp.concatenate([xrow[own], xrow[par]], axis=0))
    residual = hidden_q + dot(mixed, wo[...], NN) + vecs[4:5, :]
    gain2, shift2 = vecs[2:3, :], vecs[3:4, :]
    hat2, rstd2 = normalise(residual)
    normed2 = (hat2 * gain2 + shift2).astype(BF)
    cotangent = jnp.concatenate([cot2[0], cot2[1]], axis=0)
    half = ff // 2
    unit_result = residual + vecs[5:6, :]
    grad_normed2 = jnp.zeros((nq, d), F32)
    for j in range(ff // step):
        units = pl.ds(j * step, step)
        up_bias = jnp.concatenate([bias[(j * step) // half, 2 + (j * step) % half // 256 + i : 3 + (j * step) % half // 256 + i, :] for i in range(step // 256)], axis=1)
        inner = dot(normed2, up[:, units], NN) + up_bias
        square = inner * inner
        bent = jnp.tanh(GELU_C * inner * (1.0 + GELU_A * square))
        activated = (0.5 * inner * (1.0 + bent)).astype(BF)
        unit_result = unit_result + dot(activated, down[units, :], NN)
        slope = 0.5 * (1.0 + bent) + 0.5 * inner * (1.0 - bent * bent) * (
            GELU_C * (1.0 + 3.0 * GELU_A * square)
        )
        grad_inner = (dot(cotangent, down[units, :], NT) * slope).astype(BF)
        grad_normed2 = grad_normed2 + dot(grad_inner, up[:, units], NT)
        down_grad = dot(activated, cotangent, TN).astype(BF)
        up_grad = dot(normed2, grad_inner, TN).astype(BF)
        m, r = (j * step) // half, (j * step) % half
        for b in range(2):
            wg[m, pl.ds(UP_AT + 2 * r + b * d, d), :] = up_grad[:, b * 256 : (b + 1) * 256]
            wg[m, pl.ds(DOWN_AT + b * half + r, step), :] = down_grad[:, b * 256 : (b + 1) * 256]
        sv[6 + j : 7 + j, :] = column_sum(grad_inner.astype(F32))
    out = unit_result.astype(BF)
    result2[0] = out[:BLOCK]
    result2[1] = out[BLOCK:]
    cot_f = cotangent.astype(F32)
    grad_residual = cot_f + normalise_back(grad_normed2 * gain2, hat2, rstd2)
    sv[2:3, :] = column_sum(grad_normed2 * hat2)
    sv[3:4, :] = column_sum(grad_normed2)
    sv[4:5, :] = column_sum(grad_residual)
    sv[5:6, :] = column_sum(cot_f)
    branch_grad = grad_residual.astype(BF)
    out_grad = dot(mixed, branch_grad, TN).astype(BF)
    for m in range(2):
        for b in range(2):
            wg[m, pl.ds(OUT_AT + b * 256, 256), :] = out_grad[m * 256 : (m + 1) * 256, b * 256 : (b + 1) * 256]
    grad_mixed = dot(branch_grad, wo[...], NT).astype(BF).astype(F32) * live
    att[...] = grad_mixed

    def back(p, carry):
        at = lanes_of(p)
        query = split_heads(q_ref[:, at])
        query_wide = jnp.concatenate([query, other2], axis=1)
        heads = att[:, at]
        grads = split_heads(heads)
        product = jnp.transpose(heads) * att_t[p]
        delta = jnp.concatenate([column_sum(product[:HEAD_DIM]), column_sum(product[HEAD_DIM:])], axis=1)
        log_total = lse[p][0:1, :]
        query_grad = jnp.zeros((PAIR, 2 * nq), F32)
        for c in range(steps):
            keys = k_ref[chunk(c), at]
            scores = dot(jnp.concatenate([keys, hot[chunk(c), :]], axis=1), query_wide, NT)
            probs = jnp.exp(scores - log_total)
            grad_probs = dot(v_ref[chunk(c), at], grads, NT)
            grad_scores = (probs * (grad_probs - delta)).astype(BF)
            dk_ref[chunk(c), at] = dot(grad_scores, query, NN).astype(BF)
            dv_ref[chunk(c), at] = dot(probs.astype(BF), grads, NN).astype(BF)
            query_grad = query_grad + dot(keys, grad_scores, TN)
        joined = join_heads_t(query_grad) * (1.0 / math.sqrt(HEAD_DIM))
        dq_ref[:, at] = jnp.transpose(joined).astype(BF)
        return carry

    lax.fori_loop(0, pairs, back, 0)

    dwk[...] = jnp.zeros_like(dwk)
    dwv[...] = jnp.zeros_like(dwv)

    def tokens_back(grad_normed, block):
        hat, rstd = normalise(hidden_of(block))
        return (
            normalise_back(grad_normed * gain, hat, rstd),
            column_sum(grad_normed * hat),
            column_sum(grad_normed),
        )

    def project_back(c, carry):
        gain_sum, shift_sum, token_sum, value_sum = carry
        at = pl.ds(pl.multiple_of(c * step, step), step)
        low, key_grad, value_grad = normed[at, :], dk_ref[at, :], dv_ref[at, :]
        dwk[...] += dot(low, key_grad, TN)
        dwv[...] += dot(low, value_grad, TN)
        grad_normed = dot(key_grad, wk[...], NT) + dot(value_grad, wv[...], NT)
        token_grad, a, b = tokens_back(grad_normed, xrow[pl.ds(c * nb, nb)].reshape(step, d))
        t_buf[pl.ds(c * nb, nb)] = token_grad.reshape(nb, BLOCK, d)
        return (
            gain_sum + a,
            shift_sum + b,
            token_sum + column_sum(token_grad),
            value_sum + column_sum(value_grad.astype(F32)),
        )

    zero = jnp.zeros((1, d), F32)
    gain_sum, shift_sum, token_sum, value_sum = lax.fori_loop(0, steps, project_back, (zero,) * 4)
    query_grad = dq_ref[...]
    token_grad, a, b = tokens_back(
        dot(query_grad, wq[...], NT), jnp.concatenate([xrow[own], xrow[par]], axis=0)
    )
    token_grad = token_grad + grad_residual
    t_buf[own] += token_grad[:BLOCK]
    t_buf[par] += token_grad[BLOCK:]
    for i in range(t_out.shape[0]):
        t_out[i] = t_buf[i].astype(BF)
    sv[0:1, :] = gain_sum + a
    sv[1:2, :] = shift_sum + b
    sv[10:11, :] = column_sum(query_grad.astype(F32))
    sv[11:12, :] = value_sum
    sv[12:16, :] = jnp.zeros((4, d), F32)
    sv[12:13, :] = ids[...]
    sv[SV_TABLE:, :] = jnp.zeros((sv.shape[0] - SV_TABLE, d), F32)
    slot = lax.broadcasted_iota(jnp.int32, (sv.shape[0] - SV_TABLE, d), 0) == 2 * dp + lax.div(seq, 4)
    sv[SV_TABLE:, :] = jnp.where(slot, token_sum + column_sum(token_grad), 0.0)
    query_weight_grad = dot(query_rows(normed), query_grad, TN).astype(BF)
    for m in range(2):
        at = slice(m * 256, (m + 1) * 256)
        wg[m, pl.ds(Q_AT, d), :] = query_weight_grad[:, at]
        wg[m, pl.ds(K_AT, d), :] = dwk[:, at].astype(BF)
        wg[m, pl.ds(V_AT, d), :] = dwv[:, at].astype(BF)


def layer(xrow, seg_all, cot2, embed, vecs, wq, wk, wv, wo, up, down, bias, ids, sv_rows):
    shape = jax.ShapeDtypeStruct
    blocks, _, d = xrow.shape
    length = blocks * BLOCK
    nq = 2 * BLOCK
    pairs = d // PAIR
    return pl.pallas_call(
        layer_kernel,
        out_shape=(
            shape(cot2.shape, BF),
            shape((2, WG_ROWS, 256), BF),
            shape((sv_rows, d), F32),
            shape((blocks, BLOCK, d), BF),
        ),
        in_specs=vmem_spec(13),
        out_specs=tuple(vmem_spec(4)),
        scratch_shapes=[
            pltpu.VMEM((length, d), BF),
            pltpu.VMEM((length, d), BF),
            pltpu.VMEM((length, d), BF),
            pltpu.VMEM((length, BLOCK), BF),
            pltpu.VMEM((length, 2 * nq), F32),
            pltpu.VMEM((nq, d), F32),
            pltpu.VMEM((pairs, PAIR, nq), F32),
            pltpu.VMEM((pairs, 8, 2 * nq), F32),
            pltpu.VMEM((nq, d), BF),
            pltpu.VMEM((length, d), BF),
            pltpu.VMEM((length, d), BF),
            pltpu.VMEM((nq, d), BF),
            pltpu.VMEM((blocks, BLOCK, d), F32),
            pltpu.VMEM((d, d), F32),
            pltpu.VMEM((d, d), F32),
        ],
        compiler_params=pltpu.CompilerParams(vmem_limit_bytes=60 << 20),
        name="layer",
    )(xrow, seg_all, cot2, embed, vecs, wq, wk, wv, wo, up, down, bias, ids)


def reduce_kernel(
    orders, wg, sv, t_in, result2,
    wg_out, sv_out, tg_out, res_out,
    acc, core_buf, step_buf, t_core, t_acc, t_step, sv_buf, sv_acc, send_sem, recv_sem,
):
    dp, seq, mp = here()
    g = lax.div(seq, 4)
    y, zl = bit(seq, 1), bit(seq, 2)
    dims = orders[0]
    greet(("core",) + tuple(sorted(dims)))
    wire = Wire(send_sem, recv_sem)
    part = WG_ROWS // len(orders)
    piece = 256

    def add_rows(out, out_at, a, a_at, b, b_at, n):
        size = min(piece, n)

        def one(i, carry):
            def at(base):
                return pl.ds(pl.multiple_of(base + i * size, size), size)

            out[at(out_at), :] = a[at(a_at), :] + b[at(b_at), :]
            return carry

        lax.fori_loop(0, n // size, one, 0)

    def weights_chain(n):
        low, size = n * part, part
        at = pl.ds(low, size)
        copy = wire.send(wg.at[1 - mp, at], core_buf.at[at], "core")
        yield
        copy.wait_recv()
        add_rows(acc, low, wg.at[mp], low, core_buf, low, size)
        used = n * part
        for i, dim in enumerate(orders[n]):
            half = size // 2
            b = side(dim)
            spot = pl.ds(used, half)
            there = pl.ds(pl.multiple_of(low + (1 - b) * half, half), half)
            copy = wire.send(acc.at[there], step_buf.at[spot], dim)
            yield
            copy.wait_recv()
            low = low + b * half
            size = half
            last = i == len(orders[n]) - 1
            add_rows(wg_out if last else acc, low, acc, low, step_buf, used, size)
            used += half
        for dim in reversed(orders[n]):
            at = pl.ds(pl.multiple_of(low, size), size)
            copy = wire.send(wg_out.at[at], wg_out.at[at], dim)
            yield
            copy.wait_recv()
            low = low - side(dim) * size
            size = 2 * size

    def vectors_chain():
        sv_acc[0] = sv[...]
        for i, dim in enumerate(("core",) + tuple(dims)):
            copy = wire.send(sv_acc.at[i], sv_buf.at[i], dim)
            yield
            copy.wait_recv()
            sv_acc[i + 1] = sv_acc[i] + sv_buf[i]
        sv_out[...] = sv_acc[len(dims) + 1]

    def tokens_chain():
        copy = wire.send(t_in.at[:, :, :, 1 - mp], t_core, "core")
        back = wire.send(result2.at[1], res_out.at[g], "zh")
        res_out[g] = result2[0]
        yield
        copy.wait_recv()
        for a in range(2):
            for b in range(2):
                for c in range(2):
                    t_acc[a, b, c] = t_in[a, b, c, mp] + t_core[a, b, c]
        one = wire.send(t_acc.at[0, :, 1 - y], t_step.at[0], "y")
        two = wire.send(t_acc.at[1, 1 - zl], t_step.at[1], "zl")
        yield
        one.wait_recv()
        for i in range(2):
            t_acc[0, i, y] += t_step[0, i]
        one = wire.send(t_acc.at[0, 1 - zl, y], t_step.at[2, 0], "zl")
        two.wait_recv()
        for i in range(2):
            t_acc[1, zl, i] += t_step[1, i]
        two = wire.send(t_acc.at[1, zl, 1 - y], t_step.at[2, 1], "y")
        yield
        one.wait_recv()
        two.wait_recv()
        t_acc[0, zl, y] += t_step[2, 0]
        t_acc[1, zl, y] += t_step[2, 1]
        copy = wire.send(t_acc.at[1 - g, zl, y], tg_out.at[g], "zh")
        tg_out[g] = t_acc[g, zl, y]
        yield
        copy.wait_recv()
        back.wait_recv()

    chains = [weights_chain(n) for n in range(len(orders))] + [tokens_chain(), vectors_chain()]
    while chains:
        running = []
        for chain in chains:
            try:
                next(chain)
                running.append(chain)
            except StopIteration:
                pass
        chains = running
    wire.finish()


def reduce(wg, sv, t_in, result2, orders):
    shape = jax.ShapeDtypeStruct
    block = t_in.shape[-2:]
    dims = len(orders[0])
    copies = len(orders) * (2 * dims + 1) + 7 + dims + 1
    return pl.pallas_call(
        functools.partial(reduce_kernel, orders),
        out_shape=(
            shape((WG_ROWS, 256), BF),
            shape(sv.shape, F32),
            shape(result2.shape, BF),
            shape(result2.shape, BF),
        ),
        in_specs=vmem_spec(4),
        out_specs=tuple(vmem_spec(4)),
        scratch_shapes=[
            pltpu.VMEM((WG_ROWS, 256), BF),
            pltpu.VMEM((WG_ROWS, 256), BF),
            pltpu.VMEM((WG_ROWS, 256), BF),
            pltpu.VMEM((2, 2, 2) + block, BF),
            pltpu.VMEM((2, 2, 2) + block, BF),
            pltpu.VMEM((3, 2) + block, BF),
            pltpu.VMEM((dims + 1,) + sv.shape, F32),
            pltpu.VMEM((dims + 2,) + sv.shape, F32),
            pltpu.SemaphoreType.DMA((copies,)),
            pltpu.SemaphoreType.DMA((copies,)),
        ],
        compiler_params=pltpu.CompilerParams(
            collective_id=1, has_side_effects=True, vmem_limit_bytes=60 << 20
        ),
        name="reduce",
    )(wg, sv, t_in, result2)


def local(
    n_dp, tokens, segments, timesteps, step_table, first_gain, first_shift, query_weight, query_bias,
    key_weight, value_weight, value_bias, out_weight, out_bias, second_gain, second_shift,
    up_weight, up_bias, down_weight, down_bias, cotangent,
):
    dp, seq, mp = here()
    g = lax.div(seq, 4)
    d = tokens.shape[2]
    table_rows = tokens.shape[0] * n_dp
    segs = jnp.broadcast_to(segments.astype(F32)[:, None, :], (segments.shape[0], 8, segments.shape[1]))
    bias = jnp.concatenate([query_bias, value_bias, up_bias, jnp.zeros((512,), BF)]).astype(F32).reshape(8, 256)
    step = lax.dynamic_index_in_dim(timesteps, g, 0, keepdims=False)
    embed = lax.dynamic_slice_in_dim(step_table, step, 1, 0).astype(F32)
    vecs = jnp.stack(
        [first_gain, first_shift, second_gain, second_shift, out_bias.astype(F32), down_bias.astype(F32)]
        + [jnp.zeros_like(first_gain)] * 2
    )
    speaks = (lax.rem(seq, 4) == 0) & (mp == 0)
    ids = jnp.where((jnp.arange(d) == 2 * dp + g) & speaks, step, 0).astype(F32)[None, :]
    xrow, seg_all, cot2, wq, wk, wv, wo, up, down, bias_all = gather(
        tokens, cotangent, segs, query_weight, key_weight, value_weight, out_weight, up_weight, down_weight, bias
    )
    sv_rows = SV_TABLE + -(-table_rows // 8) * 8
    result2, wg, sv, t_out = layer(
        xrow, seg_all, cot2, embed, vecs, wq, wk, wv, wo, up, down, bias_all, ids, sv_rows
    )
    orders = [["x", "y", "zl", "zh"], ["y", "zl", "zh", "x"], ["zl", "x", "y", "zh"]]
    if n_dp != 2:
        orders = [[dim for dim in order if dim != "x"] for order in orders]
    wg, sv, token_grad, result = reduce(wg, sv, t_out.reshape((2, 2, 2, 2) + t_out.shape[1:]), result2, orders)
    if n_dp != 2:
        wg, sv = lax.psum((wg.astype(F32), sv), "dp")
    wide = wg.astype(F32)

    def blocks(at, rows, n):
        return jnp.concatenate([wide[at + i * rows : at + (i + 1) * rows] for i in range(n)], axis=1)

    ids = sv[12, :table_rows].astype(jnp.int32)
    picks = (jnp.arange(step_table.shape[0], dtype=jnp.int32)[:, None] == ids[None, :]).astype(F32)
    table_grad = jnp.dot(picks, sv[SV_TABLE : SV_TABLE + table_rows], precision=lax.Precision.HIGHEST)
    half, units = query_weight.shape[1], up_weight.shape[1]

    def mine(row, width):
        return lax.dynamic_slice_in_dim(row, mp * width, width, 0)

    return (
        result,
        token_grad.astype(F32),
        table_grad,
        sv[0],
        sv[1],
        wide[Q_AT:K_AT],
        mine(sv[10], half),
        wide[K_AT:V_AT],
        wide[V_AT:],
        mine(sv[11], half),
        blocks(OUT_AT, out_weight.shape[0], 2),
        sv[4],
        sv[2],
        sv[3],
        blocks(UP_AT, d, 4),
        mine(sv[6:10].reshape(-1), units),
        blocks(DOWN_AT, units, 2),
        sv[5],
    )


def solution(mesh):
    rows, chars, whole = P("dp", ("seq", "mp"), None), P("dp", ("seq", "mp")), P()
    columns, split, tall = P(None, "mp"), P("mp"), P("mp", None)
    in_specs = (
        rows, chars, P("dp"), whole, whole, whole, columns, split, columns, columns, split, tall,
        whole, whole, whole, columns, split, tall, whole, rows,
    )
    out_specs = (
        rows, rows, whole, whole, whole, columns, split, columns, columns, split, tall,
        whole, whole, whole, columns, split, tall, whole,
    )
    return jax.shard_map(
        functools.partial(local, mesh.shape["dp"]),
        mesh=mesh,
        in_specs=in_specs,
        out_specs=out_specs,
        check_vma=False,
    )
```

time: 714 us -> 270 us (0.38)
  waiting for transfers between devices: 452 us -> 0 us
  Pallas kernels: 0 us -> 247 us
  blocking collectives: 117 us -> 0 us
  matrix products: 67.2 us -> 2.24 us
  local copies, waits for them, and re-layouts: 35.7 us -> 9.24 us
  other arithmetic: 26.1 us -> 8.84 us
  between operations: 14.5 us -> 2.79 us
    psum x2 -> x0, waiting for transfers between devices: 269 us -> none  [the longest x1 137 us: local(): lax.psum((table_grad, grad_gain_first, grad_shift_first, out_bias_term, g...]
    pallas_call x0 -> x3, Pallas kernels: none -> 247 us  [the longest x1 110 us: gather(): pl.pallas_call(gather_kernel, out_shape=(shape((blocks, BLOCK, d), BF), s...]
    reduce_scatter x5 -> x0, waiting for transfers between devices: 109 us -> none  [the longest x1 84.9 us: local(): lax.psum_scatter(pair_parts.astype(jnp.bfloat16), 'seq', scatter_dimensio...]
    psum x2 -> x0, blocking collectives: 83.4 us -> none  [the longest x1 45.4 us: local(): lax.psum((proj_grads, bias_pair, grad_out, unit_grads[0], unit_grads[1],...]
    all_gather x2 -> x0, waiting for transfers between devices: 73 us -> none  [the longest x1 46.6 us: local(): lax.all_gather(values, 'seq', axis=1, tiled=True)]
    dot_general x28 -> x1, matrix products: 67.2 us -> 2.24 us  [local(): jnp.dot(picks, sv[SV_TABLE:SV_TABLE + table_rows], precision=lax.Precisio...]
    all_gather x6 -> x0, blocking collectives: 33.3 us -> none  [the longest x1 22.1 us: local(): lax.all_gather(seg_all, 'seq', axis=1, tiled=True)]
    reduce_sum x12 -> x0, other arithmetic: 17.2 us -> none  [the longest x2 5 us: attend_one_row(): total_row = total_row * factor + jnp.sum(weights, axis=-1)]
  transfers between devices with their start and end apart: 9 -> 0, of which waited for: 8 -> 0; matrix products, arithmetic and copies ran while one was open for 4% -> 0% of each run, Pallas kernels for 0% -> 0%
where the time goes in v1:
time: 270 us
  Pallas kernels  247 us (91%)
  local copies, waits for them, and re-layouts  9.24 us (3%)
  other arithmetic  8.84 us (3%)
  between operations  2.79 us (1%)
    pallas_call x1, Pallas kernels, gather(): pl.pallas_call(gather_kernel, out_shape=(shape((blocks, BLOCK, d), BF), s...  110 us
    pallas_call x1, Pallas kernels, reduce(): pl.pallas_call(functools.partial(reduce_kernel, orders), out_shape=(shape...  93.1 us
    pallas_call x1, Pallas kernels, layer(): pl.pallas_call(layer_kernel, out_shape=(shape(cot2.shape, BF), shape((2,...  44 us

profile of v1, /device:TPU:0, one launch (start us, length us, event | category | flops | bytes accessed | tf_op | source)
XLA Modules:
  0.0 270.0 jit_solution(11242022855592959444)
XLA Ops:
  0.7 0.0 copy-start.8
  0.7 0.0 copy-start.9
  0.7 0.0 copy-start.4
  0.7 0.0 copy-start.5
  0.7 0.0 copy-start.6
  0.7 0.0 copy-start.7
  0.7 1.3 dynamic_slice.20
  3.9 1.3 dynamic-slice_convert_fusion.embed
  5.2 1.2 fusion.3.ids
  6.5 0.7 maximum_convert_fusion
  7.2 0.6 reshape.67.bias
  7.8 0.7 convert_element_type.36
  8.4 0.6 broadcast_in_dim.20.segs
  9.0 109.8 %gather.1 = (bf16[16,128,512]{2,1,0:T(8,128)(2,1)}, f32[16,8,128]{2,1,0:T(8,128)}, bf16[2,128,512]{2,1,0:T(8,128)(2,1)}, bf16[512,512]{1,0:T(8,128)(2,1)}, bf16[...) custom-call(bf16[2,128,512]{2,1,0:T(8,128)(2,1)} %tokens.1, ...), custom_call_target="tpu_custom_call" | custom-call | tf_op jit(solution)/shard_map/gather/pallas_call | solution.py:181
  118.8 0.0 copy-done.8
  118.9 0.0 copy-done.9
  118.9 0.0 copy-done.4
  118.9 0.0 copy-done.5
  118.9 0.0 copy-done.6
  118.9 0.0 copy-done.7
  118.9 0.6 stack.39.vecs
  119.6 44.0 %layer.1 = (bf16[2,128,512]{2,1,0:T(8,128)(2,1)}, bf16[2,6144,256]{2,1,0:T(8,128)(2,1)}, f32[24,512]{1,0:T(8,128)}, bf16[16,128,512]{2,1,0:T(8,128)(2,1)}) custom-call(bf16[16,128,512]{2,1,0:T(8,128)(2,1)} %get-tuple-element.36.xrow, f32[16,8,128]{2,1,0:T(8,128)} %get-tuple-element.37.seg_all, bf16[2,128,512]{2,1,0:T(8,128)(2,1)} %get-tuple-element.38.cot2, ...), custom_call_target="tpu_custom_call" | custom-call | tf_op jit(solution)/shard_map/layer/pallas_call | solution.py:457
  163.5 93.1 %reduce.1 = (bf16[6144,256]{1,0:T(8,128)(2,1)}, f32[24,512]{1,0:T(8,128)}, bf16[2,128,512]{2,1,0:T(8,128)(2,1)}, bf16[2,128,512]{2,1,0:T(8,128)(2,1)}) custom-call(bf16[2,6144,256]{2,1,0:T(8,128)(2,1)} %get-tuple-element.46.wg, f32[24,512]{1,0:T(8,128)} %get-tuple-element.47.sv, bf16[2,2,2,2,128,512]{5,4,3,2,1,0:T(8,128)(2,1)} %bitcast.21, ...), custom_call_target="tpu_custom_call" | custom-call | tf_op jit(solution)/shard_map/reduce/pallas_call | solution.py:603
  256.7 1.4 fusion.4
  258.1 0.0 copy-start
  258.1 1.6 pad_maximum_fusion.1
  259.7 1.0 copy-done
  260.7 1.2 fusion.5
  261.9 1.6 pad_maximum_fusion
  263.5 0.0 copy-start.3
  263.5 0.0 copy-start.1
  263.5 0.0 copy-start.2
  263.5 0.9 pad_maximum_fusion.2
  264.4 0.0 copy-done.3
  264.4 0.6 fusion.7
  265.0 0.6 constant_dynamic-slice_fusion
  265.6 2.2 fusion
  267.8 0.0 copy-done.1
  267.8 0.9 convert_element_type.41
  268.7 0.6 dynamic_slice.26
  269.3 0.0 copy-done.2
  269.3 0.7 copy.40
  (8 shorter events, 0.1 us)
Async XLA Ops:
  0.7 118.2 %copy-start.8 = (bf16[512]{0:T(512)(128)(2,1)S(1)}, bf16[512]{0:T(512)(128)(2,1)}, u32[]{:S(2)}) copy-start(bf16[512]{0:T(512)(128)(2,1)} %param.32) | copy-start | bytes 3076
  0.7 118.2 %copy-start.9 = (bf16[512]{0:T(512)(128)(2,1)S(1)}, bf16[512]{0:T(512)(128)(2,1)}, u32[]{:S(2)}) copy-start(bf16[512]{0:T(512)(128)(2,1)} %param.38) | copy-start | bytes 3076
  0.7 118.2 %copy-start.4 = (f32[512]{0:T(512)S(1)}, f32[512]{0:T(512)}, u32[]{:S(2)}) copy-start(f32[512]{0:T(512)} %param.24) | copy-start | bytes 6148
  0.7 118.2 %copy-start.5 = (f32[512]{0:T(512)S(1)}, f32[512]{0:T(512)}, u32[]{:S(2)}) copy-start(f32[512]{0:T(512)} %param.25) | copy-start | bytes 6148
  0.7 118.2 %copy-start.6 = (f32[512]{0:T(512)S(1)}, f32[512]{0:T(512)}, u32[]{:S(2)}) copy-start(f32[512]{0:T(512)} %param.33) | copy-start | bytes 6148
  0.7 118.2 %copy-start.7 = (f32[512]{0:T(512)S(1)}, f32[512]{0:T(512)}, u32[]{:S(2)}) copy-start(f32[512]{0:T(512)} %param.34) | copy-start | bytes 6148
  258.1 2.6 copy-start
  263.5 0.9 copy-start.3
  263.5 4.3 %copy-start.1 = (bf16[2,128,512]{2,1,0:T(8,128)(2,1)S(1)}, bf16[2,128,512]{2,1,0:T(8,128)(2,1)}, u32[]{:S(2)}) copy-start(bf16[2,128,512]{2,1,0:T(8,128)(2,1)} %get-tuple-element.51) | copy-start | bytes 786436
  263.5 5.8 %copy-start.2 = (bf16[2,128,512]{2,1,0:T(8,128)(2,1)S(1)}, bf16[2,128,512]{2,1,0:T(8,128)(2,1)}, u32[]{:S(2)}) copy-start(bf16[2,128,512]{2,1,0:T(8,128)(2,1)} %get-tuple-element.93) | copy-start | bytes 786436
